TPU v7x, 32 devices: a whole 2x2x4 slice. The times are simulated.
32 devices in a mesh: dp: 4 (over x, core), fsdp: 8 (over z, y).
Axes of the slice: x: 2, y: 2, z: 4, core: 2. Of those that a mesh axis runs over, the one named last changes fastest.
Arguments:
- hidden: bfloat16 [4096, 8192], P(('dp', 'fsdp')), may hold values from -6 to 6
- d_attn: bfloat16 [4096, 1024], P(('dp', 'fsdp')), may hold values from -24 to 24
- w_query: bfloat16 [8192, 1024], P('fsdp'), may hold values from -0.0625 to 0.0625
- w_key: bfloat16 [8192, 128], P('fsdp'), may hold values from -0.0625 to 0.0625
- w_value: bfloat16 [8192, 128], P('fsdp'), may hold values from -0.0625 to 0.0625
- cache_keys: bfloat16 [2048, 128], P('fsdp'), may hold values from -700 to 700
- cache_values: bfloat16 [2048, 128], P('fsdp'), may hold values from -6 to 6
- lengths: int32 [4, 4], P('dp'), may hold values from 1 to 768, 1024 in all within a row
Outputs:
- grad_keys: float32 [2048, 128], P('fsdp')
- grad_values: float32 [2048, 128], P('fsdp')
Inputs may be any that keep to these rules, and one draw needn't show every extreme that they name: `lengths`: each row sums to 1024 and its longest conversation has exactly 768 tokens.
All inputs are finite; a program needn't handle non-finite values.
Results may differ from a plain program's by a relative error of at most 0.0075.
The roundings to bfloat16 on the way count: a program that leaves them out, or rounds other values in their place, can miss the bound.
Values may be sent and summed in bfloat16 or wider, within the bound.
No kernel may reach another device: no remote copies, remote signals or barrier semaphores. Data moves between devices by JAX's collectives and lax.ppermute only.
A program may use at most 128 MiB of HBM per device.

v0:
```python
import functools
import math

import jax
import jax.numpy as jnp
from jax import lax
from jax.experimental import pallas as pl
from jax.experimental.pallas import tpu as pltpu
from jax.sharding import PartitionSpec as P

F32 = jnp.float32
BF16 = jnp.bfloat16
VMEM_LIMIT = 56 * 1024 * 1024


def swap(value, axis, size, bit):
    return lax.ppermute(value, axis, [(i, i ^ bit) for i in range(size)])


def bits_down(size):
    bits = []
    bit = size // 2
    while bit:
        bits.append(bit)
        bit //= 2
    return bits


def double(block, order, axis, size, bit):
    return jnp.concatenate([block, swap(block, axis, size, bit)]), order + [o ^ bit for o in order]


def finish(block, order, axis, size, bits):
    for bit in bits[:-1]:
        block, order = double(block, order, axis, size, bit)
    return [block, swap(block, axis, size, bits[-1])], order + [o ^ bits[-1] for o in order]


def together(*values):
    return lax.optimization_barrier(values)


def params():
    return pltpu.CompilerParams(vmem_limit_bytes=VMEM_LIMIT)


def run_copies(copies):
    for copy in copies:
        copy.start()
    for copy in copies:
        copy.wait()


def prepare(where, hidden, w_query, w_key, w_value, n_dp, n_fsdp):
    inner = n_fsdp // 2
    tokens = hidden.shape[0]
    rows_w, q_width = w_query.shape
    head_dim = w_key.shape[1]
    share = rows_w // n_dp

    def body(where_ref, hidden_ref, wq_ref, wk_ref, wv_ref, *rest):
        sent, part_kv, part_q, sems = rest[: inner - 1], rest[-3], rest[-2], rest[-1]
        me, dp = where_ref[0], where_ref[1]
        rows = pl.ds(pl.multiple_of(dp * share, 16), share)
        pairs = [
            (wk_ref.at[rows], part_kv.at[:, pl.ds(0, head_dim)]),
            (wv_ref.at[rows], part_kv.at[:, pl.ds(head_dim, head_dim)]),
            (wq_ref.at[rows], part_q),
        ]
        for k in range(1, inner):
            for side, bit in enumerate((0, inner)):
                start = pl.multiple_of((me ^ k ^ bit) * rows_w, 128)
                pairs.append(
                    (hidden_ref.at[:, pl.ds(start, rows_w)], sent[k - 1].at[:, pl.ds(side * rows_w, rows_w)])
                )
        run_copies([pltpu.make_async_copy(a, b, sems.at[i]) for i, (a, b) in enumerate(pairs)])

    moved = 2 * (tokens * 2 * rows_w * 2 * (inner - 1) + share * (q_width + 2 * head_dim) * 2)
    out = pl.pallas_call(
        body,
        in_specs=[pl.BlockSpec(memory_space=pltpu.SMEM)] + [pl.BlockSpec(memory_space=pl.ANY)] * 4,
        out_specs=[pl.BlockSpec(memory_space=pltpu.VMEM)] * (inner + 1),
        out_shape=[jax.ShapeDtypeStruct((tokens, 2 * rows_w), BF16)] * (inner - 1)
        + [
            jax.ShapeDtypeStruct((share, 2 * head_dim), BF16),
            jax.ShapeDtypeStruct((share, q_width), BF16),
        ],
        scratch_shapes=[pltpu.SemaphoreType.DMA((3 + 2 * (inner - 1),))],
        compiler_params=params(),
        cost_estimate=pl.CostEstimate(flops=0, bytes_accessed=moved, transcendentals=0),
        name="prepare",
    )(where, hidden, w_query, w_key, w_value)
    return out[: inner - 1], out[-2], out[-1]


def multiply(where, hidden, received, near, far, order, n_fsdp, groups):
    inner = n_fsdp // 2
    tokens = hidden.shape[0]
    slots, share, cols = far[0].shape
    n_dp = slots * len(far)
    rows_w = n_dp * share
    step = 256 if all(g % 256 == 0 for g in groups) else 128
    n_in = inner - 1 + len(near) + len(far)

    def body(where_ref, hidden_ref, *rest):
        blocks, rest = rest[: inner - 1], rest[inner - 1 :]
        near_refs, rest = rest[: len(near)], rest[len(near) :]
        far_refs, rest = rest[: len(far)], rest[len(far) :]
        outs = rest[:-3]
        x_all, w_all, sems = rest[-3:]
        me, dp = where_ref[0], where_ref[1]
        pairs = []
        for side, bit in enumerate((0, inner)):
            start = pl.multiple_of((me ^ bit) * rows_w, 128)
            pairs.append(
                (
                    hidden_ref.at[:, pl.ds(start, rows_w)],
                    x_all.at[pl.ds(0, tokens), pl.ds(side * rows_w, rows_w)],
                )
            )
        for k in range(1, inner):
            pairs.append((blocks[k - 1], x_all.at[pl.ds(k * tokens, tokens)]))
        to = 0
        for ref, (_, start, wide) in zip(near_refs, near):
            pairs.append((ref.at[:, pl.ds(start, wide)], w_all.at[pl.ds(0, rows_w), pl.ds(to, wide)]))
            to += wide
        for slot, o in enumerate(order):
            to = pl.multiple_of(rows_w + (dp ^ o) * share, 16)
            pairs.append((far_refs[slot // slots].at[slot % slots], w_all.at[pl.ds(to, share)]))
        run_copies([pltpu.make_async_copy(a, b, sems.at[i]) for i, (a, b) in enumerate(pairs)])

        base = 0
        for g, wide in enumerate(groups):

            @pl.loop(0, wide // step)
            def _(n, g=g, base=base):
                at = pl.multiple_of(n * step, 128)
                product = jnp.dot(
                    x_all[...], w_all[:, pl.ds(base + at, step)], preferred_element_type=F32
                )
                for k in range(inner):
                    outs[g * inner + k][:, pl.ds(at, step)] = product[k * tokens : (k + 1) * tokens]

            base += wide

    copies = 2 + (inner - 1) + len(near) + n_dp
    moved = inner * tokens * 2 * rows_w * 2 + 2 * rows_w * cols * 2 + inner * tokens * cols * 4
    out = pl.pallas_call(
        body,
        in_specs=[pl.BlockSpec(memory_space=pltpu.SMEM)]
        + [pl.BlockSpec(memory_space=pl.ANY)] * (1 + n_in),
        out_specs=[pl.BlockSpec(memory_space=pltpu.VMEM)] * (inner * len(groups)),
        out_shape=[jax.ShapeDtypeStruct((tokens, g), F32) for g in groups for _ in range(inner)],
        scratch_shapes=[
            pltpu.VMEM((inner * tokens, 2 * rows_w), BF16),
            pltpu.VMEM((2 * rows_w, cols), BF16),
            pltpu.SemaphoreType.DMA((copies,)),
        ],
        compiler_params=params(),
        cost_estimate=pl.CostEstimate(
            flops=2 * inner * tokens * 2 * rows_w * cols, bytes_accessed=moved, transcendentals=0
        ),
        name="multiply",
    )(where, hidden, *received, *[array for array, _, _ in near], *far)
    return [list(out[g * inner : (g + 1) * inner]) for g in range(len(groups))]


def attend(where, lengths, partials, d_attn, cache, c_order, group, g_order):
    tokens = d_attn.shape[0]
    n_blocks, block, head_dim = cache[0].shape
    slots = n_blocks // len(group)
    n_convs = lengths.shape[1]
    scale = head_dim ** (-0.5)
    to_log2 = scale * math.log2(math.e)
    n_heads = d_attn.shape[1] // head_dim
    pair = 2 if n_heads % 2 == 0 else 1
    lanes = pair * tokens
    n_cache = n_blocks * block
    n_group = n_blocks * tokens
    chunk = 512
    n_part = sum(len(terms) for terms in partials)

    def body(where_ref, len_ref, d_ref, *rest):
        cache_refs, rest = rest[:2], rest[2:]
        group_refs, rest = rest[: len(group)], rest[len(group) :]
        part_refs = list(rest[:n_part])
        keep_ref, give_ref, gk, gv, s_ref, p_ref, q_ref, ck_ref, cv_ref = rest[n_part:]
        me, dp = where_ref[0], where_ref[1]
        even = dp % 2 == 0

        @pl.when(even)
        def _():
            ck_ref[...] = cache_refs[0][...]
            cv_ref[...] = cache_refs[1][...]

        @pl.when(jnp.logical_not(even))
        def _():
            ck_ref[...] = cache_refs[1][...]
            cv_ref[...] = cache_refs[0][...]

        h = 0
        for terms in partials:
            refs, part_refs = part_refs[: len(terms)], part_refs[len(terms) :]
            for at in range(0, terms[0].shape[1], head_dim):
                q = refs[0][:, at : at + head_dim]
                for ref in refs[1:]:
                    q = q + ref[:, at : at + head_dim]
                q_ref[h, 0] = q.astype(BF16)
                q_ref[h, 1] = d_ref[:, h * head_dim : (h + 1) * head_dim]
                h += 1

        q_pos = me * tokens + lax.broadcasted_iota(jnp.int32, (1, lanes), 1) % tokens
        begin = jnp.zeros((1, lanes), jnp.int32)
        end = jnp.int32(0)
        for i in range(n_convs):
            end = end + len_ref[0, i]
            begin = jnp.where(end <= q_pos, end, begin)

        @pl.loop(0, n_heads // pair)
        def _(step):
            rows_q = jnp.concatenate([q_ref[step * pair + i, 0] for i in range(pair)], axis=0)
            rows_d = jnp.concatenate([q_ref[step * pair + i, 1] for i in range(pair)], axis=0)
            dims = (((1,), (1,)), ((), ()))
            top = jnp.full((1, lanes), -jnp.inf, F32)
            cache_spans = [
                (b, r, min(chunk, block)) for b in range(n_blocks) for r in range(0, block, min(chunk, block))
            ]
            for b, r, size in cache_spans:
                s = lax.dot_general(
                    ck_ref[b, r : r + size], rows_q, dims, preferred_element_type=F32
                )
                s_ref[pl.ds(b * block + r, size)] = s
                top = jnp.maximum(top, jnp.max(s, axis=0, keepdims=True))
            for b in range(n_blocks):
                s = lax.dot_general(group_refs[b // slots][b % slots, :, :head_dim], rows_q, dims, preferred_element_type=F32)
                pos = (me ^ g_order[b]) * tokens + lax.broadcasted_iota(jnp.int32, (tokens, lanes), 0)
                s = jnp.where((pos <= q_pos) & (pos >= begin), s, -jnp.inf)
                s_ref[pl.ds(n_cache + b * tokens, tokens)] = s
                top = jnp.maximum(top, jnp.max(s, axis=0, keepdims=True))
            total = jnp.zeros((1, lanes), F32)
            for r in range(0, n_cache + n_group, chunk):
                e = jnp.exp2((s_ref[pl.ds(r, chunk)] - top) * to_log2)
                s_ref[pl.ds(r, chunk)] = e
                total = total + jnp.sum(e, axis=0, keepdims=True)
            inv = 1.0 / total
            delta = jnp.zeros((1, lanes), F32)
            for b in range(n_blocks):
                p = s_ref[pl.ds(n_cache + b * tokens, tokens)] * inv
                dp_ = lax.dot_general(group_refs[b // slots][b % slots, :, head_dim:], rows_d, dims, preferred_element_type=F32)
                delta = delta + jnp.sum(p.astype(BF16).astype(F32) * dp_, axis=0, keepdims=True)
            for b, r, size in cache_spans:
                at = pl.ds(b * block + r, size)
                p = s_ref[at] * inv
                pb = p.astype(BF16)
                dp_ = lax.dot_general(
                    cv_ref[b, r : r + size], rows_d, dims, preferred_element_type=F32
                )
                s_ref[at] = p
                p_ref[at] = dp_
                delta = delta + jnp.sum(pb.astype(F32) * dp_, axis=0, keepdims=True)
                g = jnp.dot(pb, rows_d, preferred_element_type=F32)
                gv[at] = jnp.where(step == 0, 0.0, gv[at]) + g
            for b, r, size in cache_spans:
                at = pl.ds(b * block + r, size)
                ds = (s_ref[at] * (p_ref[at] - delta)).astype(BF16)
                g = jnp.dot(ds, rows_q, preferred_element_type=F32)
                gk[at] = jnp.where(step == 0, 0.0, gk[at]) + g

        @pl.when(even)
        def _():
            keep_ref[...] = gk[...] * scale
            give_ref[...] = gv[...]

        @pl.when(jnp.logical_not(even))
        def _():
            keep_ref[...] = gv[...]
            give_ref[...] = gk[...] * scale

    rows = n_heads * tokens
    flops = 2 * rows * head_dim * (5 * n_cache + 2 * n_group)
    return pl.pallas_call(
        body,
        in_specs=[pl.BlockSpec(memory_space=pltpu.SMEM)] * 2
        + [pl.BlockSpec(memory_space=pltpu.VMEM)] * (3 + len(group) + n_part),
        out_specs=[pl.BlockSpec(memory_space=pltpu.VMEM)] * 2,
        out_shape=[jax.ShapeDtypeStruct((n_cache, head_dim), F32)] * 2,
        scratch_shapes=[
            pltpu.VMEM((n_cache, head_dim), F32),
            pltpu.VMEM((n_cache, head_dim), F32),
            pltpu.VMEM((n_cache + n_group, lanes), F32),
            pltpu.VMEM((n_cache, lanes), F32),
            pltpu.VMEM((n_heads, 2, tokens, head_dim), BF16),
            pltpu.VMEM((n_blocks, block, head_dim), BF16),
            pltpu.VMEM((n_blocks, block, head_dim), BF16),
        ],
        compiler_params=params(),
        cost_estimate=pl.CostEstimate(
            flops=flops,
            bytes_accessed=12 * n_cache * head_dim,
            transcendentals=rows * (n_cache + n_group),
        ),
        name="attend",
    )(where, lengths, d_attn, *cache, *group, *[term for terms in partials for term in terms])


def make_on_device(n_dp, n_fsdp):
    inner = n_fsdp // 2

    def on_device(hidden, d_attn, w_query, w_key, w_value, cache_keys, cache_values, lengths):
        me = lax.axis_index("fsdp")
        dp = lax.axis_index("dp")
        where = jnp.stack([me, dp]).astype(jnp.int32)
        head_dim = w_key.shape[1]
        q_width = w_query.shape[1]
        even = dp % 2 == 0
        f_bits, d_bits = bits_down(n_fsdp), bits_down(n_dp)

        def from_owners(products):
            return [products[0]] + [swap(x, "fsdp", n_fsdp, k + 1) for k, x in enumerate(products[1:])]

        sent, part_kv, part_q = prepare(where, hidden, w_query, w_key, w_value, n_dp, n_fsdp)
        received = [swap(block, "fsdp", n_fsdp, k + 1) for k, block in enumerate(sent)]
        part_q = swap(part_q, "fsdp", n_fsdp, inner)
        part_kv = swap(part_kv, "fsdp", n_fsdp, inner)
        far_kv, order = double(part_kv[None], [0], "dp", n_dp, d_bits[0])
        middle = part_q.shape[0] // 2
        halves = [swap(part_q[:middle], "dp", n_dp, d_bits[0]), swap(part_q[middle:], "dp", n_dp, d_bits[0])]
        cache = jnp.where(even, cache_keys, cache_values)[None]
        tied = together(part_q, *halves, far_kv, cache, *received)
        part_q, halves, far_kv, cache, received = tied[0], tied[1:3], tied[3], tied[4], tied[5:]
        far_q = jnp.stack([part_q, jnp.concatenate(halves)])
        far_q, d_order = finish(far_q, order, "dp", n_dp, d_bits[1:])
        far_kv, _ = finish(far_kv, order, "dp", n_dp, d_bits[1:])
        near_kv = [(w_key, 0, head_dim), (w_value, 0, head_dim)]
        (out_kv,) = multiply(
            where, hidden, received, near_kv, far_kv, d_order, n_fsdp, (2 * head_dim,)
        )
        cache, f_order = double(cache, [0], "fsdp", n_fsdp, f_bits[0])
        far_q[1], cache, out_kv[0] = together(far_q[1], cache, out_kv[0])
        parts_kv = from_owners(out_kv)
        own = functools.reduce(lambda a, b: a + b, parts_kv).astype(BF16)
        group = [own] + [swap(own, "fsdp", n_fsdp, k) for k in range(1, inner)]
        (out_q,) = multiply(
            where, hidden, received, [(w_query, 0, q_width)], far_q, d_order, n_fsdp, (q_width,)
        )
        for bit in f_bits[1:]:
            cache, f_order = double(cache, f_order, "fsdp", n_fsdp, bit)
        tied = together(cache, *out_q, *group)
        cache, out_q, group = tied[0], tied[1 : 1 + inner], tied[1 + inner :]
        g_order = [o for o in f_order if o < inner]
        group = jnp.stack([group[o] for o in g_order])
        group, g_order = finish(group, g_order, "fsdp", n_fsdp, [inner])
        parts_q = from_owners(out_q)
        cache = (cache, swap(cache, "dp", n_dp, 1))

        keep, give = attend(where, lengths, [parts_q], d_attn, cache, f_order, group, g_order)

        half = keep + swap(give, "dp", n_dp, 1)
        size = half.shape[0] // n_fsdp
        mine = half[:size]
        for slot in range(1, n_fsdp):
            out = half[slot * size : (slot + 1) * size].astype(BF16)
            mine = mine + swap(out, "fsdp", n_fsdp, f_order[slot]).astype(F32)
        for bit in bits_down(n_dp)[:-2]:
            mine = mine + swap(mine, "dp", n_dp, bit)
        beside, other, across = (swap(mine, "dp", n_dp, bit) for bit in (2, 1, 3))
        mine = mine + beside
        other = other + across
        return jnp.where(even, mine, other), jnp.where(even, other, mine)

    return on_device


def solution(mesh):
    placed = (
        P(("dp", "fsdp"), None),
        P(("dp", "fsdp"), None),
        P("fsdp", None),
        P("fsdp", None),
        P("fsdp", None),
        P("fsdp", None),
        P("fsdp", None),
        P("dp", None),
    )
    return jax.shard_map(
        make_on_device(mesh.shape["dp"], mesh.shape["fsdp"]),
        mesh=mesh,
        in_specs=placed,
        out_specs=(P("fsdp", None), P("fsdp", None)),
        check_vma=False,
    )
```

profile of v0, /device:TPU:0, one launch (start us, length us, event | category | flops | bytes accessed | tf_op | source)
XLA Modules:
  0.0 164.3 jit_solution(12898685846243792248)
XLA Ops:
  1.3 3.8 %prepare.1 = (bf16[128,2048]{1,0:T(8,128)(2,1)}, bf16[128,2048]{1,0:T(8,128)(2,1)}, bf16[128,2048]{1,0:T(8,128)(2,1)}, bf16[256,256]{1,0:T(8,128)(2,1)}, bf16[256,1024]{1,0:T(8,128)(2,1)}) custom-call(s32[2]{0:T(128)} %pad_add_fusion.where_ref, bf16[128,8192]{1,0:T(8,128)(2,1)} %hidden_ref.5, bf16[1024,1024]{1,0:T(8,128)(2,1)} %rest_3_.3, ...), custom_call_target="tpu_custom_call" | custom-call | bytes 4456448 | tf_op jit(solution)/shard_map/prepare/pallas_call | solution.py:79
  5.1 4.1 %collective-permute-start = (bf16[256,1024]{1,0:T(8,128)(2,1)}, bf16[256,1024]{1,0:T(8,128)(2,1)S(1)}, u32[]{:S(2)}, u32[]{:S(2)}) collective-permute-start(bf16[256,1024]{1,0:T(8,128)(2,1)} %get-tuple-element.37), channel_id=1, source_target_pairs={{0,4},{1,5},{2,6},{3,7},{4,0},{5,1},{6,2},{7,3},{8,12},{9,13},{10,... | collective-permute-start | bytes 1572872 | tf_op jit(solution)/shard_map/ppermute | solution.py:17
  12.7 25.5 %collective-permute-done.3 = bf16[256,256]{1,0:T(8,128)(2,1)S(1)} collective-permute-done((bf16[256,256]{1,0:T(8,128)(2,1)}, bf16[256,256]{1,0:T(8,128)(2,1)S(1)}, u32[]{:S(2)}, u32[]{:S(2)}) %collective-permute-start.3) | collective-permute-done | bytes 131104 | tf_op jit(solution)/shard_map/ppermute | solution.py:17
  40.4 4.3 %collective-permute-done.4 = bf16[1,256,256]{2,1,0:T(8,128)(2,1)S(1)} collective-permute-done((bf16[1,256,256]{2,1,0:T(8,128)(2,1)S(1)}, bf16[1,256,256]{2,1,0:T(8,128)(2,1)S(1)}, u32[]{:S(2)}, u32[]{:S(2)}) %collective-permute-start.4) | collective-permute-done | bytes 131104 | tf_op jit(solution)/shard_map/ppermute | solution.py:17
  48.2 2.1 %collective-permute-done.2 = bf16[128,1024]{1,0:T(8,128)(2,1)S(1)} collective-permute-done((bf16[128,1024]{1,0:T(8,128)(2,1)S(1)}, bf16[128,1024]{1,0:T(8,128)(2,1)S(1)}, u32[]{:S(2)}, u32[]{:S(2)}) %collective-permute-start.2) | collective-permute-done | bytes 262176 | tf_op jit(solution)/shard_map/ppermute | solution.py:17
  50.3 3.8 %collective-permute-done.1 = bf16[128,1024]{1,0:T(8,128)(2,1)S(1)} collective-permute-done((bf16[128,1024]{1,0:T(8,128)(2,1)S(1)}, bf16[128,1024]{1,0:T(8,128)(2,1)S(1)}, u32[]{:S(2)}, u32[]{:S(2)}) %collective-permute-start.1) | collective-permute-done | bytes 262176 | tf_op jit(solution)/shard_map/ppermute | solution.py:17
  54.9 5.2 %collective-permute-done.9 = bf16[1,256,128]{2,1,0:T(8,128)(2,1)S(1)} collective-permute-done((bf16[1,256,128]{2,1,0:T(8,128)(2,1)S(1)}, bf16[1,256,128]{2,1,0:T(8,128)(2,1)S(1)}, u32[]{:S(2)}, u32[]{:S(2)}) %collective-permute-start.9) | collective-permute-done | bytes 65568 | tf_op jit(solution)/shard_map/ppermute | solution.py:17
  60.8 4.0 %multiply.2 = (f32[128,256]{1,0:T(8,128)}, f32[128,256]{1,0:T(8,128)}, f32[128,256]{1,0:T(8,128)}, f32[128,256]{1,0:T(8,128)}) custom-call(s32[2]{0:T(128)} %pad_add_fusion.where_ref, bf16[128,8192]{1,0:T(8,128)(2,1)} %hidden_ref.5, bf16[128,2048]{1,0:T(8,128)(2,1)} %copy-done.2, bf16[128,2048]{1,0:T(8,128)(2,1)} %copy-done.3, bf16[128,2048]{1,0:T(8,128)(2,1)} %copy-done.4, ...), custom_call_target="tpu_custom_call" | custom-call | flops 536870912 | bytes 3670016 | tf_op jit(solution)/shard_map/multiply/pallas_call | solution.py:148
  64.8 2.1 %collective-permute-start.11 = (bf16[2,256,128]{2,1,0:T(8,128)(2,1)S(1)}, bf16[2,256,128]{2,1,0:T(8,128)(2,1)S(1)}, u32[]{:S(2)}, u32[]{:S(2)}) collective-permute-start(bf16[2,256,128]{2,1,0:T(8,128)(2,1)S(1)} %pad_maximum_fusion.5), channel_id=1, source_target_pairs={{0,2},{1,3},{2,0},{3,1},{4,6},{5,7},{6,4},{7,5},{8,10},{9,11},{10,... | collective-permute-start | bytes 393224 | tf_op jit(solution)/shard_map/ppermute | solution.py:17
  68.5 1.9 %collective-permute-start.15 = (f32[128,256]{1,0:T(8,128)}, f32[128,256]{1,0:T(8,128)S(1)}, u32[]{:S(2)}, u32[]{:S(2)}) collective-permute-start(f32[128,256]{1,0:T(8,128)} %get-tuple-element.60), channel_id=1, source_target_pairs={{0,3},{1,2},{2,1},{3,0},{4,7},{5,6},{6,5},{7,4},{8,11},{9,10},{10,... | collective-permute-start | bytes 393224 | tf_op jit(solution)/shard_map/ppermute | solution.py:17
  70.7 2.0 %collective-permute-start.12 = (bf16[4,256,128]{2,1,0:T(8,128)(2,1)S(1)}, bf16[4,256,128]{2,1,0:T(8,128)(2,1)S(1)}, u32[]{:S(2)}, u32[]{:S(2)}) collective-permute-start(bf16[4,256,128]{2,1,0:T(8,128)(2,1)S(1)} %pad_maximum_fusion.3), channel_id=1, source_target_pairs={{0,1},{1,0},{2,3},{3,2},{4,5},{5,4},{6,7},{7,6},{8,9},{9,8},{10,11... | collective-permute-start | bytes 786440 | tf_op jit(solution)/shard_map/ppermute | solution.py:17
  74.4 2.4 %collective-permute-done.15 = f32[128,256]{1,0:T(8,128)S(1)} collective-permute-done((f32[128,256]{1,0:T(8,128)}, f32[128,256]{1,0:T(8,128)S(1)}, u32[]{:S(2)}, u32[]{:S(2)}) %collective-permute-start.15) | collective-permute-done | bytes 131104 | tf_op jit(solution)/shard_map/ppermute | solution.py:17
  81.3 7.7 %multiply.3 = (f32[128,1024]{1,0:T(8,128)}, f32[128,1024]{1,0:T(8,128)}, f32[128,1024]{1,0:T(8,128)}, f32[128,1024]{1,0:T(8,128)}) custom-call(s32[2]{0:T(128)} %pad_add_fusion.where_ref, bf16[128,8192]{1,0:T(8,128)(2,1)} %hidden_ref.5, bf16[128,2048]{1,0:T(8,128)(2,1)} %copy-done.2, bf16[128,2048]{1,0:T(8,128)(2,1)} %copy-done.3, ...), custom_call_target="tpu_custom_call" | custom-call | flops 2147483648 | bytes 8388608 | tf_op jit(solution)/shard_map/multiply/pallas_call | solution.py:148
  92.7 2.6 %collective-permute-start.20 = (bf16[4,128,256]{2,1,0:T(8,128)(2,1)S(1)}, bf16[4,128,256]{2,1,0:T(8,128)(2,1)S(1)}, u32[]{:S(2)}, u32[]{:S(2)}) collective-permute-start(bf16[4,128,256]{2,1,0:T(8,128)(2,1)S(1)} %pad_maximum_fusion.4.rest_2_), channel_id=1, source_target_pairs={{0,4},{1,5},{2,6},{3,7},{4,0},{5,1},{6,2},{7,3},{8,12},{9,13},{10,... | collective-permute-start | bytes 786440 | tf_op jit(solution)/shard_map/ppermute | solution.py:17
  95.3 22.1 %collective-permute-done.20.rest_3_ = bf16[4,128,256]{2,1,0:T(8,128)(2,1)S(1)} collective-permute-done((bf16[4,128,256]{2,1,0:T(8,128)(2,1)S(1)}, bf16[4,128,256]{2,1,0:T(8,128)(2,1)S(1)}, u32[]{:S(2)}, u32[]{:S(2)}) %collective-permute-start.20) | collective-permute-done | bytes 262176 | tf_op jit(solution)/shard_map/ppermute | solution.py:17
  120.9 14.0 %attend.1 = (f32[2048,128]{1,0:T(8,128)}, f32[2048,128]{1,0:T(8,128)}) custom-call(s32[2]{0:T(128)} %pad_add_fusion.where_ref, s32[1,4]{1,0:T(1,128)} %len_ref.1, bf16[128,1024]{1,0:T(8,128)(2,1)} %d_ref.1, bf16[8,256,128]{2,1,0:T(8,128)(2,1)} %copy-done.5, bf16[8,256,128]{2,1,0:T(8,128)(2,1)} %copy-done.14, bf16[4,128,256]{2,1,0:T(8,128)(2,1)} %copy-done.7, ...), custom_call_target="tpu_custom_call" | custom-call | flops 3221225472 | bytes 3145728 | tf_op jit(solution)/shard_map/attend/pallas_call | solution.py:281
  134.9 2.9 %collective-permute-done.24 = f32[2048,128]{1,0:T(8,128)S(1)} collective-permute-done((f32[2048,128]{1,0:T(8,128)}, f32[2048,128]{1,0:T(8,128)S(1)}, u32[]{:S(2)}, u32[]{:S(2)}) %collective-permute-start.24) | collective-permute-done | bytes 1048608 | tf_op jit(solution)/shard_map/ppermute | solution.py:17
  139.1 2.0 %collective-permute-start.25 = (bf16[256,128]{1,0:T(8,128)(2,1)S(1)}, bf16[256,128]{1,0:T(8,128)(2,1)S(1)}, u32[]{:S(2)}, u32[]{:S(2)}) collective-permute-start(bf16[256,128]{1,0:T(8,128)(2,1)S(1)} %get-tuple-element.76), channel_id=1, source_target_pairs={{0,4},{1,5},{2,6},{3,7},{4,0},{5,1},{6,2},{7,3},{8,12},{9,13},{10,... | collective-permute-start | bytes 196616 | tf_op jit(solution)/shard_map/ppermute | solution.py:17
  141.2 3.1 %collective-permute-start.31 = (bf16[256,128]{1,0:T(8,128)(2,1)S(1)}, bf16[256,128]{1,0:T(8,128)(2,1)S(1)}, u32[]{:S(2)}, u32[]{:S(2)}) collective-permute-start(bf16[256,128]{1,0:T(8,128)(2,1)S(1)} %get-tuple-element.77), channel_id=1, source_target_pairs={{0,7},{1,6},{2,5},{3,4},{4,3},{5,2},{6,1},{7,0},{8,15},{9,14},{10,... | collective-permute-start | bytes 196616 | tf_op jit(solution)/shard_map/ppermute | solution.py:17
  144.3 2.6 %collective-permute-start.29 = (bf16[256,128]{1,0:T(8,128)(2,1)S(1)}, bf16[256,128]{1,0:T(8,128)(2,1)S(1)}, u32[]{:S(2)}, u32[]{:S(2)}) collective-permute-start(bf16[256,128]{1,0:T(8,128)(2,1)S(1)} %get-tuple-element.79), channel_id=1, source_target_pairs={{0,5},{1,4},{2,7},{3,6},{4,1},{5,0},{6,3},{7,2},{8,13},{9,12},{10,... | collective-permute-start | bytes 196616 | tf_op jit(solution)/shard_map/ppermute | solution.py:17
  147.9 2.0 %collective-permute-start.27 = (bf16[256,128]{1,0:T(8,128)(2,1)S(1)}, bf16[256,128]{1,0:T(8,128)(2,1)S(1)}, u32[]{:S(2)}, u32[]{:S(2)}) collective-permute-start(bf16[256,128]{1,0:T(8,128)(2,1)S(1)} %get-tuple-element.81), channel_id=1, source_target_pairs={{0,6},{1,7},{2,4},{3,5},{4,2},{5,3},{6,0},{7,1},{8,14},{9,15},{10,... | collective-permute-start | bytes 196616 | tf_op jit(solution)/shard_map/ppermute | solution.py:17
  150.2 2.9 %collective-permute-done.29 = bf16[256,128]{1,0:T(8,128)(2,1)S(1)} collective-permute-done((bf16[256,128]{1,0:T(8,128)(2,1)S(1)}, bf16[256,128]{1,0:T(8,128)(2,1)S(1)}, u32[]{:S(2)}, u32[]{:S(2)}) %collective-permute-start.29) | collective-permute-done | bytes 65568 | tf_op jit(solution)/shard_map/ppermute | solution.py:17
  157.1 3.6 %collective-permute-done.34 = f32[256,128]{1,0:T(8,128)S(1)} collective-permute-done((f32[256,128]{1,0:T(8,128)S(1)}, f32[256,128]{1,0:T(8,128)S(1)}, u32[]{:S(2)}, u32[]{:S(2)}) %collective-permute-start.34) | collective-permute-done | bytes 131104 | tf_op jit(solution)/shard_map/ppermute | solution.py:17
  160.7 2.8 %collective-permute-done.32 = f32[256,128]{1,0:T(8,128)S(1)} collective-permute-done((f32[256,128]{1,0:T(8,128)S(1)}, f32[256,128]{1,0:T(8,128)S(1)}, u32[]{:S(2)}, u32[]{:S(2)}) %collective-permute-start.32) | collective-permute-done | bytes 131104 | tf_op jit(solution)/shard_map/ppermute | solution.py:17
  (97 shorter events, 33.8 us)
Async XLA Ops:
  5.1 34.7 %collective-permute-start = (bf16[256,1024]{1,0:T(8,128)(2,1)}, bf16[256,1024]{1,0:T(8,128)(2,1)S(1)}, u32[]{:S(2)}, u32[]{:S(2)}) collective-permute-start(bf16[256,1024]{1,0:T(8,128)(2,1)} %get-tuple-element.37), channel_id=1, source_target_pairs={{0,4},{1,5},{2,6},{3,7},{4,0},{5,1},{6,2},{7,3},{8,12},{9,13},{10,... | collective-permute-start | bytes 1572872 | tf_op jit(solution)/shard_map/ppermute | solution.py:17
  9.2 29.1 %collective-permute-start.3 = (bf16[256,256]{1,0:T(8,128)(2,1)}, bf16[256,256]{1,0:T(8,128)(2,1)S(1)}, u32[]{:S(2)}, u32[]{:S(2)}) collective-permute-start(bf16[256,256]{1,0:T(8,128)(2,1)} %get-tuple-element.38), channel_id=1, source_target_pairs={{0,4},{1,5},{2,6},{3,7},{4,0},{5,1},{6,2},{7,3},{8,12},{9,13},{10,... | collective-permute-start | bytes 393224 | tf_op jit(solution)/shard_map/ppermute | solution.py:17
  9.3 37.1 %collective-permute-start.5 = (bf16[128,2048]{1,0:T(8,128)(2,1)}, bf16[128,2048]{1,0:T(8,128)(2,1)S(1)}, u32[]{:S(2)}, u32[]{:S(2)}) collective-permute-start(bf16[128,2048]{1,0:T(8,128)(2,1)} %get-tuple-element.39), channel_id=1, source_target_pairs={{0,1},{1,0},{2,3},{3,2},{4,5},{5,4},{6,7},{7,6},{8,9},{9,8},{10,11... | collective-permute-start | bytes 1572872 | tf_op jit(solution)/shard_map/ppermute | solution.py:17
  11.0 35.3 %collective-permute-start.6 = (bf16[128,2048]{1,0:T(8,128)(2,1)}, bf16[128,2048]{1,0:T(8,128)(2,1)S(1)}, u32[]{:S(2)}, u32[]{:S(2)}) collective-permute-start(bf16[128,2048]{1,0:T(8,128)(2,1)} %get-tuple-element.40), channel_id=1, source_target_pairs={{0,2},{1,3},{2,0},{3,1},{4,6},{5,7},{6,4},{7,5},{8,10},{9,11},{10,... | collective-permute-start | bytes 1572872 | tf_op jit(solution)/shard_map/ppermute | solution.py:17
  12.6 35.6 %collective-permute-start.7 = (bf16[128,2048]{1,0:T(8,128)(2,1)}, bf16[128,2048]{1,0:T(8,128)(2,1)S(1)}, u32[]{:S(2)}, u32[]{:S(2)}) collective-permute-start(bf16[128,2048]{1,0:T(8,128)(2,1)} %get-tuple-element.41), channel_id=1, source_target_pairs={{0,3},{1,2},{2,1},{3,0},{4,7},{5,6},{6,5},{7,4},{8,11},{9,10},{10,... | collective-permute-start | bytes 1572872 | tf_op jit(solution)/shard_map/ppermute | solution.py:17
  38.3 6.4 %collective-permute-start.4 = (bf16[1,256,256]{2,1,0:T(8,128)(2,1)S(1)}, bf16[1,256,256]{2,1,0:T(8,128)(2,1)S(1)}, u32[]{:S(2)}, u32[]{:S(2)}) collective-permute-start(bf16[1,256,256]{2,1,0:T(8,128)(2,1)S(1)} %bitcast.14), channel_id=1, source_target_pairs={{0,16},{8,24},{16,0},{24,8},{1,17},{9,25},{17,1},{25,9},{2,18},{10... | collective-permute-start | bytes 393224 | tf_op jit(solution)/shard_map/ppermute | solution.py:17
  39.8 10.5 %collective-permute-start.2 = (bf16[128,1024]{1,0:T(8,128)(2,1)S(1)}, bf16[128,1024]{1,0:T(8,128)(2,1)S(1)}, u32[]{:S(2)}, u32[]{:S(2)}) collective-permute-start(bf16[128,1024]{1,0:T(8,128)(2,1)S(1)} %get-tuple-element.83), channel_id=1, source_target_pairs={{0,16},{8,24},{16,0},{24,8},{1,17},{9,25},{17,1},{25,9},{2,18},{10... | collective-permute-start | bytes 786440 | tf_op jit(solution)/shard_map/ppermute | solution.py:17
  44.7 9.4 %collective-permute-start.1 = (bf16[128,1024]{1,0:T(8,128)(2,1)S(1)}, bf16[128,1024]{1,0:T(8,128)(2,1)S(1)}, u32[]{:S(2)}, u32[]{:S(2)}) collective-permute-start(bf16[128,1024]{1,0:T(8,128)(2,1)S(1)} %get-tuple-element.84), channel_id=1, source_target_pairs={{0,16},{8,24},{16,0},{24,8},{1,17},{9,25},{17,1},{25,9},{2,18},{10... | collective-permute-start | bytes 786440 | tf_op jit(solution)/shard_map/ppermute | solution.py:17
  54.3 10.5 %collective-permute-start.8 = (bf16[2,256,1024]{2,1,0:T(8,128)(2,1)S(1)}, bf16[2,256,1024]{2,1,0:T(8,128)(2,1)S(1)}, u32[]{:S(2)}, u32[]{:S(2)}) collective-permute-start(bf16[2,256,1024]{2,1,0:T(8,128)(2,1)S(1)} %pad_maximum_fusion.rest_4_), channel_id=1, source_target_pairs={{0,8},{8,0},{16,24},{24,16},{1,9},{9,1},{17,25},{25,17},{2,10},{10... | collective-permute-start | bytes 3145736 | tf_op jit(solution)/shard_map/ppermute | solution.py:17
  68.5 8.3 %collective-permute-start.15 = (f32[128,256]{1,0:T(8,128)}, f32[128,256]{1,0:T(8,128)S(1)}, u32[]{:S(2)}, u32[]{:S(2)}) collective-permute-start(f32[128,256]{1,0:T(8,128)} %get-tuple-element.60), channel_id=1, source_target_pairs={{0,3},{1,2},{2,1},{3,0},{4,7},{5,6},{6,5},{7,4},{8,11},{9,10},{10,... | collective-permute-start | bytes 393224 | tf_op jit(solution)/shard_map/ppermute | solution.py:17
  70.7 18.3 %collective-permute-start.12 = (bf16[4,256,128]{2,1,0:T(8,128)(2,1)S(1)}, bf16[4,256,128]{2,1,0:T(8,128)(2,1)S(1)}, u32[]{:S(2)}, u32[]{:S(2)}) collective-permute-start(bf16[4,256,128]{2,1,0:T(8,128)(2,1)S(1)} %pad_maximum_fusion.3), channel_id=1, source_target_pairs={{0,1},{1,0},{2,3},{3,2},{4,5},{5,4},{6,7},{7,6},{8,9},{9,8},{10,11... | collective-permute-start | bytes 786440 | tf_op jit(solution)/shard_map/ppermute | solution.py:17
  77.7 11.4 %collective-permute-start.18 = (bf16[128,256]{1,0:T(8,128)(2,1)S(1)}, bf16[128,256]{1,0:T(8,128)(2,1)S(1)}, u32[]{:S(2)}, u32[]{:S(2)}) collective-permute-start(bf16[128,256]{1,0:T(8,128)(2,1)S(1)} %add_convert_fusion), channel_id=1, source_target_pairs={{0,3},{1,2},{2,1},{3,0},{4,7},{5,6},{6,5},{7,4},{8,11},{9,10},{10,... | collective-permute-start | bytes 196616 | tf_op jit(solution)/shard_map/ppermute | solution.py:17
  79.5 9.6 %collective-permute-start.17 = (bf16[128,256]{1,0:T(8,128)(2,1)S(1)}, bf16[128,256]{1,0:T(8,128)(2,1)S(1)}, u32[]{:S(2)}, u32[]{:S(2)}) collective-permute-start(bf16[128,256]{1,0:T(8,128)(2,1)S(1)} %add_convert_fusion), channel_id=1, source_target_pairs={{0,2},{1,3},{2,0},{3,1},{4,6},{5,7},{6,4},{7,5},{8,10},{9,11},{10,... | collective-permute-start | bytes 196616 | tf_op jit(solution)/shard_map/ppermute | solution.py:17
  79.8 9.3 %collective-permute-start.16 = (bf16[128,256]{1,0:T(8,128)(2,1)S(1)}, bf16[128,256]{1,0:T(8,128)(2,1)S(1)}, u32[]{:S(2)}, u32[]{:S(2)}) collective-permute-start(bf16[128,256]{1,0:T(8,128)(2,1)S(1)} %add_convert_fusion), channel_id=1, source_target_pairs={{0,1},{1,0},{2,3},{3,2},{4,5},{5,4},{6,7},{7,6},{8,9},{9,8},{10,11... | collective-permute-start | bytes 196616 | tf_op jit(solution)/shard_map/ppermute | solution.py:17
  89.1 28.3 %collective-permute-start.21 = (f32[128,1024]{1,0:T(8,128)}, f32[128,1024]{1,0:T(8,128)S(1)}, u32[]{:S(2)}, u32[]{:S(2)}) collective-permute-start(f32[128,1024]{1,0:T(8,128)} %get-tuple-element.67), channel_id=1, source_target_pairs={{0,1},{1,0},{2,3},{3,2},{4,5},{5,4},{6,7},{7,6},{8,9},{9,8},{10,11... | collective-permute-start | bytes 1572872 | tf_op jit(solution)/shard_map/ppermute | solution.py:17
  89.8 27.7 %collective-permute-start.22 = (f32[128,1024]{1,0:T(8,128)}, f32[128,1024]{1,0:T(8,128)S(1)}, u32[]{:S(2)}, u32[]{:S(2)}) collective-permute-start(f32[128,1024]{1,0:T(8,128)} %get-tuple-element.68), channel_id=1, source_target_pairs={{0,2},{1,3},{2,0},{3,1},{4,6},{5,7},{6,4},{7,5},{8,10},{9,11},{10,... | collective-permute-start | bytes 1572872 | tf_op jit(solution)/shard_map/ppermute | solution.py:17
  91.4 27.9 %collective-permute-start.23 = (f32[128,1024]{1,0:T(8,128)}, f32[128,1024]{1,0:T(8,128)S(1)}, u32[]{:S(2)}, u32[]{:S(2)}) collective-permute-start(f32[128,1024]{1,0:T(8,128)} %get-tuple-element.69), channel_id=1, source_target_pairs={{0,3},{1,2},{2,1},{3,0},{4,7},{5,6},{6,5},{7,4},{8,11},{9,10},{10,... | collective-permute-start | bytes 1572872 | tf_op jit(solution)/shard_map/ppermute | solution.py:17
  92.7 26.6 %collective-permute-start.19 = (bf16[8,256,128]{2,1,0:T(8,128)(2,1)S(1)}, bf16[8,256,128]{2,1,0:T(8,128)(2,1)S(1)}, u32[]{:S(2)}, u32[]{:S(2)}) collective-permute-start(bf16[8,256,128]{2,1,0:T(8,128)(2,1)S(1)} %pad_maximum_fusion.1.rest_0_), channel_id=1, source_target_pairs={{0,8},{8,0},{16,24},{24,16},{1,9},{9,1},{17,25},{25,17},{2,10},{10... | collective-permute-start | bytes 1572872 | tf_op jit(solution)/shard_map/ppermute | solution.py:17
  92.7 24.7 %collective-permute-start.20 = (bf16[4,128,256]{2,1,0:T(8,128)(2,1)S(1)}, bf16[4,128,256]{2,1,0:T(8,128)(2,1)S(1)}, u32[]{:S(2)}, u32[]{:S(2)}) collective-permute-start(bf16[4,128,256]{2,1,0:T(8,128)(2,1)S(1)} %pad_maximum_fusion.4.rest_2_), channel_id=1, source_target_pairs={{0,4},{1,5},{2,6},{3,7},{4,0},{5,1},{6,2},{7,3},{8,12},{9,13},{10,... | collective-permute-start | bytes 786440 | tf_op jit(solution)/shard_map/ppermute | solution.py:17
  139.1 8.8 %collective-permute-start.25 = (bf16[256,128]{1,0:T(8,128)(2,1)S(1)}, bf16[256,128]{1,0:T(8,128)(2,1)S(1)}, u32[]{:S(2)}, u32[]{:S(2)}) collective-permute-start(bf16[256,128]{1,0:T(8,128)(2,1)S(1)} %get-tuple-element.76), channel_id=1, source_target_pairs={{0,4},{1,5},{2,6},{3,7},{4,0},{5,1},{6,2},{7,3},{8,12},{9,13},{10,... | collective-permute-start | bytes 196616 | tf_op jit(solution)/shard_map/ppermute | solution.py:17
  141.2 8.8 %collective-permute-start.31 = (bf16[256,128]{1,0:T(8,128)(2,1)S(1)}, bf16[256,128]{1,0:T(8,128)(2,1)S(1)}, u32[]{:S(2)}, u32[]{:S(2)}) collective-permute-start(bf16[256,128]{1,0:T(8,128)(2,1)S(1)} %get-tuple-element.77), channel_id=1, source_target_pairs={{0,7},{1,6},{2,5},{3,4},{4,3},{5,2},{6,1},{7,0},{8,15},{9,14},{10,... | collective-permute-start | bytes 196616 | tf_op jit(solution)/shard_map/ppermute | solution.py:17
  144.3 8.7 %collective-permute-start.29 = (bf16[256,128]{1,0:T(8,128)(2,1)S(1)}, bf16[256,128]{1,0:T(8,128)(2,1)S(1)}, u32[]{:S(2)}, u32[]{:S(2)}) collective-permute-start(bf16[256,128]{1,0:T(8,128)(2,1)S(1)} %get-tuple-element.79), channel_id=1, source_target_pairs={{0,5},{1,4},{2,7},{3,6},{4,1},{5,0},{6,3},{7,2},{8,13},{9,12},{10,... | collective-permute-start | bytes 196616 | tf_op jit(solution)/shard_map/ppermute | solution.py:17
  147.9 6.2 %collective-permute-start.27 = (bf16[256,128]{1,0:T(8,128)(2,1)S(1)}, bf16[256,128]{1,0:T(8,128)(2,1)S(1)}, u32[]{:S(2)}, u32[]{:S(2)}) collective-permute-start(bf16[256,128]{1,0:T(8,128)(2,1)S(1)} %get-tuple-element.81), channel_id=1, source_target_pairs={{0,6},{1,7},{2,4},{3,5},{4,2},{5,3},{6,0},{7,1},{8,14},{9,15},{10,... | collective-permute-start | bytes 196616 | tf_op jit(solution)/shard_map/ppermute | solution.py:17
  156.5 7.0 %collective-permute-start.32 = (f32[256,128]{1,0:T(8,128)S(1)}, f32[256,128]{1,0:T(8,128)S(1)}, u32[]{:S(2)}, u32[]{:S(2)}) collective-permute-start(f32[256,128]{1,0:T(8,128)S(1)} %fusion.5), channel_id=1, source_target_pairs={{0,16},{8,24},{16,0},{24,8},{1,17},{9,25},{17,1},{25,9},{2,18},{10... | collective-permute-start | bytes 393224 | tf_op jit(solution)/shard_map/ppermute | solution.py:17
  (27 other events, 294.5 us)
where the time goes:
time: 165 us; the launch traced here: 164 us
  waiting for transfers between devices  85.3 us (52%)
  starting transfers between devices  42.1 us (26%)
  Pallas kernels  29.5 us (18%)
  other arithmetic  4.01 us (2%)
  local copies, waits for them, and re-layouts  2.35 us (1%)
    ppermute x35, waiting for transfers between devices, swap(): return lax.ppermute(value, axis, [(i, i ^ bit) for i in range(size)])  85.3 us
    ppermute x35, starting transfers between devices, swap(): return lax.ppermute(value, axis, [(i, i ^ bit) for i in range(size)])  42.1 us
    pallas_call x1, Pallas kernels, attend(): pl.pallas_call(body, in_specs=[pl.BlockSpec(memory_space=pltpu.SMEM)] * 2...  14 us
    pallas_call x2, Pallas kernels, multiply(): pl.pallas_call(body, in_specs=[pl.BlockSpec(memory_space=pltpu.SMEM)] + [...  11.7 us
    pallas_call x1, Pallas kernels, prepare(): pl.pallas_call(body, in_specs=[pl.BlockSpec(memory_space=pltpu.SMEM)] + [...  3.81 us
  transfers between devices with their start and end apart: 35, of which 18 were waited for; matrix products, arithmetic and copies ran while one was open for 1% of the time, Pallas kernels for 7%

commit v1 on v0

--- a/solution.py
+++ b/solution.py
@@ -323,27 +323,28 @@
         part_q = swap(part_q, "fsdp", n_fsdp, inner)
         part_kv = swap(part_kv, "fsdp", n_fsdp, inner)
         far_kv, order = double(part_kv[None], [0], "dp", n_dp, d_bits[0])
+        cache = jnp.where(even, cache_keys, cache_values)[None]
         middle = part_q.shape[0] // 2
         halves = [swap(part_q[:middle], "dp", n_dp, d_bits[0]), swap(part_q[middle:], "dp", n_dp, d_bits[0])]
-        cache = jnp.where(even, cache_keys, cache_values)[None]
-        tied = together(part_q, *halves, far_kv, cache, *received)
-        part_q, halves, far_kv, cache, received = tied[0], tied[1:3], tied[3], tied[4], tied[5:]
-        far_q = jnp.stack([part_q, jnp.concatenate(halves)])
-        far_q, d_order = finish(far_q, order, "dp", n_dp, d_bits[1:])
-        far_kv, _ = finish(far_kv, order, "dp", n_dp, d_bits[1:])
+        far_kv, cache, halves[0], *received = together(far_kv, cache, halves[0], *received)
+        far_kv, d_order = finish(far_kv, order, "dp", n_dp, d_bits[1:])
         near_kv = [(w_key, 0, head_dim), (w_value, 0, head_dim)]
         (out_kv,) = multiply(
             where, hidden, received, near_kv, far_kv, d_order, n_fsdp, (2 * head_dim,)
         )
         cache, f_order = double(cache, [0], "fsdp", n_fsdp, f_bits[0])
-        far_q[1], cache, out_kv[0] = together(far_q[1], cache, out_kv[0])
+        part_q, cache, out_kv[0], *halves = together(part_q, cache, out_kv[0], *halves)
+        far_q = jnp.stack([part_q, jnp.concatenate(halves)])
+        far_q, _ = finish(far_q, order, "dp", n_dp, d_bits[1:])
         parts_kv = from_owners(out_kv)
+        cache, f_order = double(cache, f_order, "fsdp", n_fsdp, f_bits[1])
+        far_q[1], cache, *parts_kv = together(far_q[1], cache, *parts_kv)
         own = functools.reduce(lambda a, b: a + b, parts_kv).astype(BF16)
         group = [own] + [swap(own, "fsdp", n_fsdp, k) for k in range(1, inner)]
         (out_q,) = multiply(
             where, hidden, received, [(w_query, 0, q_width)], far_q, d_order, n_fsdp, (q_width,)
         )
-        for bit in f_bits[1:]:
+        for bit in f_bits[2:]:
             cache, f_order = double(cache, f_order, "fsdp", n_fsdp, bit)
         tied = together(cache, *out_q, *group)
         cache, out_q, group = tied[0], tied[1 : 1 + inner], tied[1 + inner :]

time: 165 us -> 163 us (0.988)
  waiting for transfers between devices: 85.3 us -> 80.7 us
  starting transfers between devices: 42.1 us -> 45.9 us
    ppermute x35, waiting for transfers between devices: 85.3 us -> 80.7 us  [swap(): return lax.ppermute(value, axis, [(i, i ^ bit) for i in range(size)])]
    ppermute x35, starting transfers between devices: 42.1 us -> 45.9 us  [swap(): return lax.ppermute(value, axis, [(i, i ^ bit) for i in range(size)])]
  transfers between devices with their start and end apart: 35 -> 35, of which waited for: 18 -> 15; matrix products, arithmetic and copies ran while one was open for 1% -> 0% of each run, Pallas kernels for 7% -> 7%
where the time goes in v1:
time: 163 us; the launch traced here: 162 us
  waiting for transfers between devices  80.7 us (50%)
  starting transfers between devices  45.9 us (28%)
  Pallas kernels  29.5 us (18%)
  other arithmetic  3.15 us (2%)
  local copies, waits for them, and re-layouts  2.19 us (1%)
    ppermute x35, waiting for transfers between devices, swap(): return lax.ppermute(value, axis, [(i, i ^ bit) for i in range(size)])  80.7 us
    ppermute x35, starting transfers between devices, swap(): return lax.ppermute(value, axis, [(i, i ^ bit) for i in range(size)])  45.9 us
    pallas_call x1, Pallas kernels, attend(): pl.pallas_call(body, in_specs=[pl.BlockSpec(memory_space=pltpu.SMEM)] * 2...  14 us
    pallas_call x2, Pallas kernels, multiply(): pl.pallas_call(body, in_specs=[pl.BlockSpec(memory_space=pltpu.SMEM)] + [...  11.7 us
    pallas_call x1, Pallas kernels, prepare(): pl.pallas_call(body, in_specs=[pl.BlockSpec(memory_space=pltpu.SMEM)] + [...  3.81 us
  transfers between devices with their start and end apart: 35, of which 15 were waited for; matrix products, arithmetic and copies ran while one was open for 0% of the time, Pallas kernels for 7%

profile of v1, /device:TPU:0, one launch (start us, length us, event | category | flops | bytes accessed | tf_op | source)
XLA Modules:
  0.0 162.4 jit_solution(17944956194724539657)
XLA Ops:
  1.3 3.8 %prepare.1 = (bf16[128,2048]{1,0:T(8,128)(2,1)}, bf16[128,2048]{1,0:T(8,128)(2,1)}, bf16[128,2048]{1,0:T(8,128)(2,1)}, bf16[256,256]{1,0:T(8,128)(2,1)}, bf16[256,1024]{1,0:T(8,128)(2,1)}) custom-call(s32[2]{0:T(128)} %pad_add_fusion.where_ref, bf16[128,8192]{1,0:T(8,128)(2,1)} %hidden_ref.5, bf16[1024,1024]{1,0:T(8,128)(2,1)} %rest_3_.3, ...), custom_call_target="tpu_custom_call" | custom-call | bytes 4456448 | tf_op jit(solution)/shard_map/prepare/pallas_call | solution.py:79
  5.1 4.1 %collective-permute-start = (bf16[256,1024]{1,0:T(8,128)(2,1)}, bf16[256,1024]{1,0:T(8,128)(2,1)S(1)}, u32[]{:S(2)}, u32[]{:S(2)}) collective-permute-start(bf16[256,1024]{1,0:T(8,128)(2,1)} %get-tuple-element.43), channel_id=1, source_target_pairs={{0,4},{1,5},{2,6},{3,7},{4,0},{5,1},{6,2},{7,3},{8,12},{9,13},{10,... | collective-permute-start | bytes 1572872 | tf_op jit(solution)/shard_map/ppermute | solution.py:17
  9.3 1.8 %collective-permute-start.4 = (bf16[128,2048]{1,0:T(8,128)(2,1)}, bf16[128,2048]{1,0:T(8,128)(2,1)S(1)}, u32[]{:S(2)}, u32[]{:S(2)}) collective-permute-start(bf16[128,2048]{1,0:T(8,128)(2,1)} %get-tuple-element.45), channel_id=1, source_target_pairs={{0,1},{1,0},{2,3},{3,2},{4,5},{5,4},{6,7},{7,6},{8,9},{9,8},{10,11... | collective-permute-start | bytes 1572872 | tf_op jit(solution)/shard_map/ppermute | solution.py:17
  12.8 25.5 %collective-permute-done.1 = bf16[256,256]{1,0:T(8,128)(2,1)S(1)} collective-permute-done((bf16[256,256]{1,0:T(8,128)(2,1)}, bf16[256,256]{1,0:T(8,128)(2,1)S(1)}, u32[]{:S(2)}, u32[]{:S(2)}) %collective-permute-start.1) | collective-permute-done | bytes 131104 | tf_op jit(solution)/shard_map/ppermute | solution.py:17
  40.5 4.3 %collective-permute-done.2 = bf16[1,256,256]{2,1,0:T(8,128)(2,1)S(1)} collective-permute-done((bf16[1,256,256]{2,1,0:T(8,128)(2,1)S(1)}, bf16[1,256,256]{2,1,0:T(8,128)(2,1)S(1)}, u32[]{:S(2)}, u32[]{:S(2)}) %collective-permute-start.2) | collective-permute-done | bytes 131104 | tf_op jit(solution)/shard_map/ppermute | solution.py:17
  44.8 3.4 %collective-permute-done.6.rest_2_ = bf16[128,2048]{1,0:T(8,128)(2,1)S(1)} collective-permute-done((bf16[128,2048]{1,0:T(8,128)(2,1)}, bf16[128,2048]{1,0:T(8,128)(2,1)S(1)}, u32[]{:S(2)}, u32[]{:S(2)}) %collective-permute-start.6) | collective-permute-done | bytes 524320 | tf_op jit(solution)/shard_map/ppermute | solution.py:17
  49.8 2.8 %collective-permute-start.7 = (bf16[1,256,128]{2,1,0:T(8,128)(2,1)S(1)}, bf16[1,256,128]{2,1,0:T(8,128)(2,1)S(1)}, u32[]{:S(2)}, u32[]{:S(2)}) collective-permute-start(bf16[1,256,128]{2,1,0:T(8,128)(2,1)S(1)} %select_bitcast_fusion), channel_id=1, source_target_pairs={{0,4},{1,5},{2,6},{3,7},{4,0},{5,1},{6,2},{7,3},{8,12},{9,13},{10,... | collective-permute-start | bytes 196616 | tf_op jit(solution)/shard_map/ppermute | solution.py:17
  52.6 2.4 %collective-permute-done.7 = bf16[1,256,128]{2,1,0:T(8,128)(2,1)S(1)} collective-permute-done((bf16[1,256,128]{2,1,0:T(8,128)(2,1)S(1)}, bf16[1,256,128]{2,1,0:T(8,128)(2,1)S(1)}, u32[]{:S(2)}, u32[]{:S(2)}) %collective-permute-start.7) | collective-permute-done | bytes 65568 | tf_op jit(solution)/shard_map/ppermute | solution.py:17
  55.9 4.0 %multiply.2 = (f32[128,256]{1,0:T(8,128)}, f32[128,256]{1,0:T(8,128)}, f32[128,256]{1,0:T(8,128)}, f32[128,256]{1,0:T(8,128)}) custom-call(s32[2]{0:T(128)} %pad_add_fusion.where_ref, bf16[128,8192]{1,0:T(8,128)(2,1)} %hidden_ref.5, bf16[128,2048]{1,0:T(8,128)(2,1)} %copy-done.2, bf16[128,2048]{1,0:T(8,128)(2,1)} %copy-done.3, bf16[128,2048]{1,0:T(8,128)(2,1)} %copy-done.4, ...), custom_call_target="tpu_custom_call" | custom-call | flops 536870912 | bytes 3670016 | tf_op jit(solution)/shard_map/multiply/pallas_call | solution.py:148
  60.1 2.4 %collective-permute-start.11 = (bf16[2,256,128]{2,1,0:T(8,128)(2,1)S(1)}, bf16[2,256,128]{2,1,0:T(8,128)(2,1)S(1)}, u32[]{:S(2)}, u32[]{:S(2)}) collective-permute-start(bf16[2,256,128]{2,1,0:T(8,128)(2,1)S(1)} %pad_maximum_fusion.5), channel_id=1, source_target_pairs={{0,2},{1,3},{2,0},{3,1},{4,6},{5,7},{6,4},{7,5},{8,10},{9,11},{10,... | collective-permute-start | bytes 393224 | tf_op jit(solution)/shard_map/ppermute | solution.py:17
  68.1 2.3 %collective-permute-done.13 = f32[128,256]{1,0:T(8,128)S(1)} collective-permute-done((f32[128,256]{1,0:T(8,128)S(1)}, f32[128,256]{1,0:T(8,128)S(1)}, u32[]{:S(2)}, u32[]{:S(2)}) %collective-permute-start.13) | collective-permute-done | bytes 131104 | tf_op jit(solution)/shard_map/ppermute | solution.py:17
  70.4 2.8 %collective-permute-done.14 = f32[128,256]{1,0:T(8,128)S(1)} collective-permute-done((f32[128,256]{1,0:T(8,128)S(1)}, f32[128,256]{1,0:T(8,128)S(1)}, u32[]{:S(2)}, u32[]{:S(2)}) %collective-permute-start.14) | collective-permute-done | bytes 131104 | tf_op jit(solution)/shard_map/ppermute | solution.py:17
  75.3 1.8 %collective-permute-start.17 = (bf16[128,256]{1,0:T(8,128)(2,1)S(1)}, bf16[128,256]{1,0:T(8,128)(2,1)S(1)}, u32[]{:S(2)}, u32[]{:S(2)}) collective-permute-start(bf16[128,256]{1,0:T(8,128)(2,1)S(1)} %add_convert_fusion), channel_id=1, source_target_pairs={{0,2},{1,3},{2,0},{3,1},{4,6},{5,7},{6,4},{7,5},{8,10},{9,11},{10,... | collective-permute-start | bytes 196616 | tf_op jit(solution)/shard_map/ppermute | solution.py:17
  77.3 7.7 %multiply.3 = (f32[128,1024]{1,0:T(8,128)}, f32[128,1024]{1,0:T(8,128)}, f32[128,1024]{1,0:T(8,128)}, f32[128,1024]{1,0:T(8,128)}) custom-call(s32[2]{0:T(128)} %pad_add_fusion.where_ref, bf16[128,8192]{1,0:T(8,128)(2,1)} %hidden_ref.5, bf16[128,2048]{1,0:T(8,128)(2,1)} %copy-done.2, bf16[128,2048]{1,0:T(8,128)(2,1)} %copy-done.3, ...), custom_call_target="tpu_custom_call" | custom-call | flops 2147483648 | bytes 8388608 | tf_op jit(solution)/shard_map/multiply/pallas_call | solution.py:148
  86.8 1.8 %collective-permute-start.22 = (f32[128,1024]{1,0:T(8,128)}, f32[128,1024]{1,0:T(8,128)S(1)}, u32[]{:S(2)}, u32[]{:S(2)}) collective-permute-start(f32[128,1024]{1,0:T(8,128)} %get-tuple-element.80), channel_id=1, source_target_pairs={{0,2},{1,3},{2,0},{3,1},{4,6},{5,7},{6,4},{7,5},{8,10},{9,11},{10,... | collective-permute-start | bytes 1572872 | tf_op jit(solution)/shard_map/ppermute | solution.py:17
  88.8 3.4 %collective-permute-start.20 = (bf16[4,128,256]{2,1,0:T(8,128)(2,1)S(1)}, bf16[4,128,256]{2,1,0:T(8,128)(2,1)S(1)}, u32[]{:S(2)}, u32[]{:S(2)}) collective-permute-start(bf16[4,128,256]{2,1,0:T(8,128)(2,1)S(1)} %pad_maximum_fusion.4.rest_2_), channel_id=1, source_target_pairs={{0,4},{1,5},{2,6},{3,7},{4,0},{5,1},{6,2},{7,3},{8,12},{9,13},{10,... | collective-permute-start | bytes 786440 | tf_op jit(solution)/shard_map/ppermute | solution.py:17
  92.2 25.0 %collective-permute-done.20.rest_3_ = bf16[4,128,256]{2,1,0:T(8,128)(2,1)S(1)} collective-permute-done((bf16[4,128,256]{2,1,0:T(8,128)(2,1)S(1)}, bf16[4,128,256]{2,1,0:T(8,128)(2,1)S(1)}, u32[]{:S(2)}, u32[]{:S(2)}) %collective-permute-start.20) | collective-permute-done | bytes 262176 | tf_op jit(solution)/shard_map/ppermute | solution.py:17
  119.1 14.0 %attend.1 = (f32[2048,128]{1,0:T(8,128)}, f32[2048,128]{1,0:T(8,128)}) custom-call(s32[2]{0:T(128)} %pad_add_fusion.where_ref, s32[1,4]{1,0:T(1,128)} %len_ref.1, bf16[128,1024]{1,0:T(8,128)(2,1)} %d_ref.1, bf16[8,256,128]{2,1,0:T(8,128)(2,1)} %copy-done.5, bf16[8,256,128]{2,1,0:T(8,128)(2,1)} %copy-done.12, bf16[4,128,256]{2,1,0:T(8,128)(2,1)} %copy-done.7, ...), custom_call_target="tpu_custom_call" | custom-call | flops 3221225472 | bytes 3145728 | tf_op jit(solution)/shard_map/attend/pallas_call | solution.py:281
  133.1 2.9 %collective-permute-done.24 = f32[2048,128]{1,0:T(8,128)S(1)} collective-permute-done((f32[2048,128]{1,0:T(8,128)}, f32[2048,128]{1,0:T(8,128)S(1)}, u32[]{:S(2)}, u32[]{:S(2)}) %collective-permute-start.24) | collective-permute-done | bytes 1048608 | tf_op jit(solution)/shard_map/ppermute | solution.py:17
  137.4 3.5 %collective-permute-start.25 = (bf16[256,128]{1,0:T(8,128)(2,1)S(1)}, bf16[256,128]{1,0:T(8,128)(2,1)S(1)}, u32[]{:S(2)}, u32[]{:S(2)}) collective-permute-start(bf16[256,128]{1,0:T(8,128)(2,1)S(1)} %get-tuple-element.88), channel_id=1, source_target_pairs={{0,4},{1,5},{2,6},{3,7},{4,0},{5,1},{6,2},{7,3},{8,12},{9,13},{10,... | collective-permute-start | bytes 196616 | tf_op jit(solution)/shard_map/ppermute | solution.py:17
  145.8 2.5 %collective-permute-start.30 = (bf16[256,128]{1,0:T(8,128)(2,1)S(1)}, bf16[256,128]{1,0:T(8,128)(2,1)S(1)}, u32[]{:S(2)}, u32[]{:S(2)}) collective-permute-start(bf16[256,128]{1,0:T(8,128)(2,1)S(1)} %get-tuple-element.90), channel_id=1, source_target_pairs={{0,3},{1,2},{2,1},{3,0},{4,7},{5,6},{6,5},{7,4},{8,11},{9,10},{10,... | collective-permute-start | bytes 196616 | tf_op jit(solution)/shard_map/ppermute | solution.py:17
  148.3 2.0 %collective-permute-start.31 = (bf16[256,128]{1,0:T(8,128)(2,1)S(1)}, bf16[256,128]{1,0:T(8,128)(2,1)S(1)}, u32[]{:S(2)}, u32[]{:S(2)}) collective-permute-start(bf16[256,128]{1,0:T(8,128)(2,1)S(1)} %get-tuple-element.89), channel_id=1, source_target_pairs={{0,7},{1,6},{2,5},{3,4},{4,3},{5,2},{6,1},{7,0},{8,15},{9,14},{10,... | collective-permute-start | bytes 196616 | tf_op jit(solution)/shard_map/ppermute | solution.py:17
  151.8 3.4 %collective-permute-done.31 = bf16[256,128]{1,0:T(8,128)(2,1)S(1)} collective-permute-done((bf16[256,128]{1,0:T(8,128)(2,1)S(1)}, bf16[256,128]{1,0:T(8,128)(2,1)S(1)}, u32[]{:S(2)}, u32[]{:S(2)}) %collective-permute-start.31) | collective-permute-done | bytes 65568 | tf_op jit(solution)/shard_map/ppermute | solution.py:17
  157.5 4.2 %collective-permute-done.32 = f32[256,128]{1,0:T(8,128)S(1)} collective-permute-done((f32[256,128]{1,0:T(8,128)S(1)}, f32[256,128]{1,0:T(8,128)S(1)}, u32[]{:S(2)}, u32[]{:S(2)}) %collective-permute-start.32) | collective-permute-done | bytes 131104 | tf_op jit(solution)/shard_map/ppermute | solution.py:17
  (105 shorter events, 29.9 us)
Async XLA Ops:
  5.1 34.7 %collective-permute-start = (bf16[256,1024]{1,0:T(8,128)(2,1)}, bf16[256,1024]{1,0:T(8,128)(2,1)S(1)}, u32[]{:S(2)}, u32[]{:S(2)}) collective-permute-start(bf16[256,1024]{1,0:T(8,128)(2,1)} %get-tuple-element.43), channel_id=1, source_target_pairs={{0,4},{1,5},{2,6},{3,7},{4,0},{5,1},{6,2},{7,3},{8,12},{9,13},{10,... | collective-permute-start | bytes 1572872 | tf_op jit(solution)/shard_map/ppermute | solution.py:17
  9.2 29.1 %collective-permute-start.1 = (bf16[256,256]{1,0:T(8,128)(2,1)}, bf16[256,256]{1,0:T(8,128)(2,1)S(1)}, u32[]{:S(2)}, u32[]{:S(2)}) collective-permute-start(bf16[256,256]{1,0:T(8,128)(2,1)} %get-tuple-element.44), channel_id=1, source_target_pairs={{0,4},{1,5},{2,6},{3,7},{4,0},{5,1},{6,2},{7,3},{8,12},{9,13},{10,... | collective-permute-start | bytes 393224 | tf_op jit(solution)/shard_map/ppermute | solution.py:17
  9.3 35.5 %collective-permute-start.4 = (bf16[128,2048]{1,0:T(8,128)(2,1)}, bf16[128,2048]{1,0:T(8,128)(2,1)S(1)}, u32[]{:S(2)}, u32[]{:S(2)}) collective-permute-start(bf16[128,2048]{1,0:T(8,128)(2,1)} %get-tuple-element.45), channel_id=1, source_target_pairs={{0,1},{1,0},{2,3},{3,2},{4,5},{5,4},{6,7},{7,6},{8,9},{9,8},{10,11... | collective-permute-start | bytes 1572872 | tf_op jit(solution)/shard_map/ppermute | solution.py:17
  11.1 33.7 %collective-permute-start.5 = (bf16[128,2048]{1,0:T(8,128)(2,1)}, bf16[128,2048]{1,0:T(8,128)(2,1)S(1)}, u32[]{:S(2)}, u32[]{:S(2)}) collective-permute-start(bf16[128,2048]{1,0:T(8,128)(2,1)} %get-tuple-element.46), channel_id=1, source_target_pairs={{0,2},{1,3},{2,0},{3,1},{4,6},{5,7},{6,4},{7,5},{8,10},{9,11},{10,... | collective-permute-start | bytes 1572872 | tf_op jit(solution)/shard_map/ppermute | solution.py:17
  12.7 35.6 %collective-permute-start.6 = (bf16[128,2048]{1,0:T(8,128)(2,1)}, bf16[128,2048]{1,0:T(8,128)(2,1)S(1)}, u32[]{:S(2)}, u32[]{:S(2)}) collective-permute-start(bf16[128,2048]{1,0:T(8,128)(2,1)} %get-tuple-element.47), channel_id=1, source_target_pairs={{0,3},{1,2},{2,1},{3,0},{4,7},{5,6},{6,5},{7,4},{8,11},{9,10},{10,... | collective-permute-start | bytes 1572872 | tf_op jit(solution)/shard_map/ppermute | solution.py:17
  39.9 8.7 %collective-permute-start.3 = (bf16[128,1024]{1,0:T(8,128)(2,1)S(1)}, bf16[128,1024]{1,0:T(8,128)(2,1)S(1)}, u32[]{:S(2)}, u32[]{:S(2)}) collective-permute-start(bf16[128,1024]{1,0:T(8,128)(2,1)S(1)} %get-tuple-element.96), channel_id=1, source_target_pairs={{0,16},{8,24},{16,0},{24,8},{1,17},{9,25},{17,1},{25,9},{2,18},{10... | collective-permute-start | bytes 786440 | tf_op jit(solution)/shard_map/ppermute | solution.py:17
  48.6 11.3 %collective-permute-start.9 = (bf16[128,1024]{1,0:T(8,128)(2,1)S(1)}, bf16[128,1024]{1,0:T(8,128)(2,1)S(1)}, u32[]{:S(2)}, u32[]{:S(2)}) collective-permute-start(bf16[128,1024]{1,0:T(8,128)(2,1)S(1)} %get-tuple-element.95), channel_id=1, source_target_pairs={{0,16},{8,24},{16,0},{24,8},{1,17},{9,25},{17,1},{25,9},{2,18},{10... | collective-permute-start | bytes 786440 | tf_op jit(solution)/shard_map/ppermute | solution.py:17
  60.0 13.1 %collective-permute-start.10 = (bf16[2,256,1024]{2,1,0:T(8,128)(2,1)S(1)}, bf16[2,256,1024]{2,1,0:T(8,128)(2,1)S(1)}, u32[]{:S(2)}, u32[]{:S(2)}) collective-permute-start(bf16[2,256,1024]{2,1,0:T(8,128)(2,1)S(1)} %pad_maximum_fusion.rest_4_), channel_id=1, source_target_pairs={{0,8},{8,0},{16,24},{24,16},{1,9},{9,1},{17,25},{25,17},{2,10},{10... | collective-permute-start | bytes 3145736 | tf_op jit(solution)/shard_map/ppermute | solution.py:17
  64.6 8.6 %collective-permute-start.14 = (f32[128,256]{1,0:T(8,128)S(1)}, f32[128,256]{1,0:T(8,128)S(1)}, u32[]{:S(2)}, u32[]{:S(2)}) collective-permute-start(f32[128,256]{1,0:T(8,128)S(1)} %copy-done.17), channel_id=1, source_target_pairs={{0,3},{1,2},{2,1},{3,0},{4,7},{5,6},{6,5},{7,4},{8,11},{9,10},{10,... | collective-permute-start | bytes 393224 | tf_op jit(solution)/shard_map/ppermute | solution.py:17
  73.2 11.8 %collective-permute-start.15 = (bf16[4,256,128]{2,1,0:T(8,128)(2,1)S(1)}, bf16[4,256,128]{2,1,0:T(8,128)(2,1)S(1)}, u32[]{:S(2)}, u32[]{:S(2)}) collective-permute-start(bf16[4,256,128]{2,1,0:T(8,128)(2,1)S(1)} %pad_maximum_fusion.3), channel_id=1, source_target_pairs={{0,1},{1,0},{2,3},{3,2},{4,5},{5,4},{6,7},{7,6},{8,9},{9,8},{10,11... | collective-permute-start | bytes 786440 | tf_op jit(solution)/shard_map/ppermute | solution.py:17
  73.7 11.4 %collective-permute-start.16 = (bf16[128,256]{1,0:T(8,128)(2,1)S(1)}, bf16[128,256]{1,0:T(8,128)(2,1)S(1)}, u32[]{:S(2)}, u32[]{:S(2)}) collective-permute-start(bf16[128,256]{1,0:T(8,128)(2,1)S(1)} %add_convert_fusion), channel_id=1, source_target_pairs={{0,1},{1,0},{2,3},{3,2},{4,5},{5,4},{6,7},{7,6},{8,9},{9,8},{10,11... | collective-permute-start | bytes 196616 | tf_op jit(solution)/shard_map/ppermute | solution.py:17
  75.3 9.8 %collective-permute-start.17 = (bf16[128,256]{1,0:T(8,128)(2,1)S(1)}, bf16[128,256]{1,0:T(8,128)(2,1)S(1)}, u32[]{:S(2)}, u32[]{:S(2)}) collective-permute-start(bf16[128,256]{1,0:T(8,128)(2,1)S(1)} %add_convert_fusion), channel_id=1, source_target_pairs={{0,2},{1,3},{2,0},{3,1},{4,6},{5,7},{6,4},{7,5},{8,10},{9,11},{10,... | collective-permute-start | bytes 196616 | tf_op jit(solution)/shard_map/ppermute | solution.py:17
  77.1 8.0 %collective-permute-start.18 = (bf16[128,256]{1,0:T(8,128)(2,1)S(1)}, bf16[128,256]{1,0:T(8,128)(2,1)S(1)}, u32[]{:S(2)}, u32[]{:S(2)}) collective-permute-start(bf16[128,256]{1,0:T(8,128)(2,1)S(1)} %add_convert_fusion), channel_id=1, source_target_pairs={{0,3},{1,2},{2,1},{3,0},{4,7},{5,6},{6,5},{7,4},{8,11},{9,10},{10,... | collective-permute-start | bytes 196616 | tf_op jit(solution)/shard_map/ppermute | solution.py:17
  85.1 32.0 %collective-permute-start.19 = (bf16[8,256,128]{2,1,0:T(8,128)(2,1)S(1)}, bf16[8,256,128]{2,1,0:T(8,128)(2,1)S(1)}, u32[]{:S(2)}, u32[]{:S(2)}) collective-permute-start(bf16[8,256,128]{2,1,0:T(8,128)(2,1)S(1)} %pad_maximum_fusion.1.rest_0_), channel_id=1, source_target_pairs={{0,8},{8,0},{16,24},{24,16},{1,9},{9,1},{17,25},{25,17},{2,10},{10... | collective-permute-start | bytes 1572872 | tf_op jit(solution)/shard_map/ppermute | solution.py:17
  85.2 31.9 %collective-permute-start.21 = (f32[128,1024]{1,0:T(8,128)}, f32[128,1024]{1,0:T(8,128)S(1)}, u32[]{:S(2)}, u32[]{:S(2)}) collective-permute-start(f32[128,1024]{1,0:T(8,128)} %get-tuple-element.79), channel_id=1, source_target_pairs={{0,1},{1,0},{2,3},{3,2},{4,5},{5,4},{6,7},{7,6},{8,9},{9,8},{10,11... | collective-permute-start | bytes 1572872 | tf_op jit(solution)/shard_map/ppermute | solution.py:17
  86.8 30.4 %collective-permute-start.22 = (f32[128,1024]{1,0:T(8,128)}, f32[128,1024]{1,0:T(8,128)S(1)}, u32[]{:S(2)}, u32[]{:S(2)}) collective-permute-start(f32[128,1024]{1,0:T(8,128)} %get-tuple-element.80), channel_id=1, source_target_pairs={{0,2},{1,3},{2,0},{3,1},{4,6},{5,7},{6,4},{7,5},{8,10},{9,11},{10,... | collective-permute-start | bytes 1572872 | tf_op jit(solution)/shard_map/ppermute | solution.py:17
  88.5 29.3 %collective-permute-start.23 = (f32[128,1024]{1,0:T(8,128)}, f32[128,1024]{1,0:T(8,128)S(1)}, u32[]{:S(2)}, u32[]{:S(2)}) collective-permute-start(f32[128,1024]{1,0:T(8,128)} %get-tuple-element.81), channel_id=1, source_target_pairs={{0,3},{1,2},{2,1},{3,0},{4,7},{5,6},{6,5},{7,4},{8,11},{9,10},{10,... | collective-permute-start | bytes 1572872 | tf_op jit(solution)/shard_map/ppermute | solution.py:17
  88.8 28.3 %collective-permute-start.20 = (bf16[4,128,256]{2,1,0:T(8,128)(2,1)S(1)}, bf16[4,128,256]{2,1,0:T(8,128)(2,1)S(1)}, u32[]{:S(2)}, u32[]{:S(2)}) collective-permute-start(bf16[4,128,256]{2,1,0:T(8,128)(2,1)S(1)} %pad_maximum_fusion.4.rest_2_), channel_id=1, source_target_pairs={{0,4},{1,5},{2,6},{3,7},{4,0},{5,1},{6,2},{7,3},{8,12},{9,13},{10,... | collective-permute-start | bytes 786440 | tf_op jit(solution)/shard_map/ppermute | solution.py:17
  137.4 8.4 %collective-permute-start.25 = (bf16[256,128]{1,0:T(8,128)(2,1)S(1)}, bf16[256,128]{1,0:T(8,128)(2,1)S(1)}, u32[]{:S(2)}, u32[]{:S(2)}) collective-permute-start(bf16[256,128]{1,0:T(8,128)(2,1)S(1)} %get-tuple-element.88), channel_id=1, source_target_pairs={{0,4},{1,5},{2,6},{3,7},{4,0},{5,1},{6,2},{7,3},{8,12},{9,13},{10,... | collective-permute-start | bytes 196616 | tf_op jit(solution)/shard_map/ppermute | solution.py:17
  140.9 7.4 %collective-permute-start.26 = (bf16[256,128]{1,0:T(8,128)(2,1)S(1)}, bf16[256,128]{1,0:T(8,128)(2,1)S(1)}, u32[]{:S(2)}, u32[]{:S(2)}) collective-permute-start(bf16[256,128]{1,0:T(8,128)(2,1)S(1)} %get-tuple-element.94), channel_id=1, source_target_pairs={{0,2},{1,3},{2,0},{3,1},{4,6},{5,7},{6,4},{7,5},{8,10},{9,11},{10,... | collective-permute-start | bytes 196616 | tf_op jit(solution)/shard_map/ppermute | solution.py:17
  142.0 8.3 %collective-permute-start.27 = (bf16[256,128]{1,0:T(8,128)(2,1)S(1)}, bf16[256,128]{1,0:T(8,128)(2,1)S(1)}, u32[]{:S(2)}, u32[]{:S(2)}) collective-permute-start(bf16[256,128]{1,0:T(8,128)(2,1)S(1)} %get-tuple-element.93), channel_id=1, source_target_pairs={{0,6},{1,7},{2,4},{3,5},{4,2},{5,3},{6,0},{7,1},{8,14},{9,15},{10,... | collective-permute-start | bytes 196616 | tf_op jit(solution)/shard_map/ppermute | solution.py:17
  143.3 7.0 %collective-permute-start.28 = (bf16[256,128]{1,0:T(8,128)(2,1)S(1)}, bf16[256,128]{1,0:T(8,128)(2,1)S(1)}, u32[]{:S(2)}, u32[]{:S(2)}) collective-permute-start(bf16[256,128]{1,0:T(8,128)(2,1)S(1)} %get-tuple-element.92), channel_id=1, source_target_pairs={{0,1},{1,0},{2,3},{3,2},{4,5},{5,4},{6,7},{7,6},{8,9},{9,8},{10,11... | collective-permute-start | bytes 196616 | tf_op jit(solution)/shard_map/ppermute | solution.py:17
  144.4 7.5 %collective-permute-start.29 = (bf16[256,128]{1,0:T(8,128)(2,1)S(1)}, bf16[256,128]{1,0:T(8,128)(2,1)S(1)}, u32[]{:S(2)}, u32[]{:S(2)}) collective-permute-start(bf16[256,128]{1,0:T(8,128)(2,1)S(1)} %get-tuple-element.91), channel_id=1, source_target_pairs={{0,5},{1,4},{2,7},{3,6},{4,1},{5,0},{6,3},{7,2},{8,13},{9,12},{10,... | collective-permute-start | bytes 196616 | tf_op jit(solution)/shard_map/ppermute | solution.py:17
  148.3 7.0 %collective-permute-start.31 = (bf16[256,128]{1,0:T(8,128)(2,1)S(1)}, bf16[256,128]{1,0:T(8,128)(2,1)S(1)}, u32[]{:S(2)}, u32[]{:S(2)}) collective-permute-start(bf16[256,128]{1,0:T(8,128)(2,1)S(1)} %get-tuple-element.89), channel_id=1, source_target_pairs={{0,7},{1,6},{2,5},{3,4},{4,3},{5,2},{6,1},{7,0},{8,15},{9,14},{10,... | collective-permute-start | bytes 196616 | tf_op jit(solution)/shard_map/ppermute | solution.py:17
  (31 other events, 293.6 us)
